TPU v7x, 32 devices: a whole 2x2x4 slice. The times are simulated.
32 devices in a mesh: opair: 4 (over y, core), vpair: 8 (over z, x).
Axes of the slice: x: 2, y: 2, z: 4, core: 2. Of those that a mesh axis runs over, the one named last changes fastest.
Arguments:
- amplitudes: bfloat16 [800, 12, 1000], P('vpair', 'opair'), may hold values from -6 to 6
- ladder_ints: bfloat16 [12, 1000, 8, 1000], P('opair', None, 'vpair'), may hold values from -0.0546875 to 0.0546875
- cycle_amps: bfloat16 [12, 100, 64], P('opair'), may hold values from -6 to 6
- cycle_ints: bfloat16 [12, 100, 100000], P('opair', None, 'vpair'), may hold values from -0.1875 to 0.1875
- occ_blocks: int32 [8], replicated, may hold values from 1 to 33, 100 in all
- virt_blocks: int32 [8], replicated, may hold values from 1 to 250, 1000 in all
- occ_start: int32 [1], replicated, may hold values from 0 to 92
- virt_start: int32 [1], replicated, may hold values from 0 to 992
- eps_occ: float32 [100], replicated, may hold values from -1 to -0.25
- eps_virt: float32 [1000], replicated, may hold values from 0.25 to 1.5
Outputs:
- update: float32 [8, 8, 100, 1000], P('opair', 'vpair')
All inputs are finite; a program needn't handle non-finite values.
Results may differ from a plain program's by a relative error of at most 0.0004.
Values may be sent and summed in bfloat16 or wider, within the bound.
A program may use at most 128 MiB of HBM per device.

v0:
```python
import jax
import jax.numpy as jnp
from jax import lax
from jax.sharding import PartitionSpec as P

NO = 100
NV = 1000
I_DEV = 2
A_DEV = 1


def irrep_of(blocks, index):
    bounds = jnp.cumsum(blocks)[:-1]
    return jnp.sum((index[:, None] >= bounds[None, :]).astype(jnp.int32), axis=1)


def shards(
    amplitudes,
    ladder_ints,
    cycle_amps,
    cycle_ints,
    occ_blocks,
    virt_blocks,
    occ_start,
    virt_start,
    eps_occ,
    eps_virt,
):
    i_win = I_DEV * lax.axis_size("opair")
    a_win = A_DEV * lax.axis_size("vpair")
    slab_depth = ladder_ints.shape[0] * ladder_ints.shape[1]
    ladder_flat = ladder_ints.reshape(slab_depth, A_DEV * NV)
    piece = lax.all_gather(amplitudes, "vpair", axis=0, tiled=True)
    ladder = jnp.dot(
        piece.reshape(piece.shape[0], slab_depth), ladder_flat, preferred_element_type=jnp.float32
    )
    ladder = ladder.reshape(i_win, NO, A_DEV, NV).transpose(0, 2, 1, 3)
    cycle = lax.dot_general(
        cycle_amps, cycle_ints, (((0, 1), (0, 1)), ((), ())), preferred_element_type=jnp.float32
    )
    cycle = cycle.reshape(i_win, a_win, cycle_ints.shape[2])
    moved = lax.all_to_all(cycle, "vpair", split_axis=1, concat_axis=2, tiled=True)
    joined = ladder + moved.reshape(i_win, A_DEV, NO, NV)
    resid = lax.psum_scatter(joined, "opair", scatter_dimension=0, tiled=True)
    first_occ = occ_start[0] + lax.axis_index("opair") * I_DEV
    first_virt = virt_start[0] + lax.axis_index("vpair") * A_DEV
    glob_i = first_occ + jnp.arange(I_DEV, dtype=jnp.int32)
    glob_a = first_virt + jnp.arange(A_DEV, dtype=jnp.int32)
    sym_i = irrep_of(occ_blocks, glob_i)
    sym_a = irrep_of(virt_blocks, glob_a)
    sym_j = irrep_of(occ_blocks, jnp.arange(NO, dtype=jnp.int32))
    sym_b = irrep_of(virt_blocks, jnp.arange(NV, dtype=jnp.int32))
    total_sym = jnp.bitwise_xor(
        jnp.bitwise_xor(sym_i[:, None, None, None], sym_a[None, :, None, None]),
        jnp.bitwise_xor(sym_j[None, None, :, None], sym_b[None, None, None, :]),
    )
    e_i = lax.dynamic_slice_in_dim(eps_occ, first_occ, I_DEV)
    e_a = lax.dynamic_slice_in_dim(eps_virt, first_virt, A_DEV)
    denom = (
        e_i[:, None, None, None]
        - e_a[None, :, None, None]
        + eps_occ[None, None, :, None]
        - eps_virt[None, None, None, :]
    )
    return jnp.where(total_sym == 0, resid / denom, jnp.float32(0.0))


def solution(mesh):
    placed = (
        P("vpair", "opair", None),
        P("opair", None, "vpair", None),
        P("opair", None, None),
        P("opair", None, "vpair"),
        P(),
        P(),
        P(),
        P(),
        P(),
        P(),
    )
    return jax.shard_map(
        shards,
        mesh=mesh,
        in_specs=placed,
        out_specs=P("opair", "vpair", None, None),
        check_vma=False,
    )
```

profile of v0, /device:TPU:5, one launch (start us, length us, event | category | flops | bytes accessed | tf_op | source)
XLA Modules:
  0.0 241.1 jit_solution(5615680304055343257)
XLA Ops:
  6.5 0.0 copy-start
  6.5 0.0 all-gather.2.cloned.1.call-start
  6.5 2.5 %copy.22 = bf16[100,3,1000]{2,1,0:T(4,128)(2,1)} copy(bf16[100,3,1000]{2,0,1:T(8,128)(2,1)} %param.10) | data formatting | bytes 1200000 | tf_op args[0]
  9.1 0.0 all-gather.2.cloned.1.call-update
  9.1 0.0 reduce-scatter.2.cloned.1.call-start
  9.1 0.0 copy-done
  9.1 4.7 %convolution_bitcast_fusion = f32[8,8,12500]{2,1,0:T(8,128)S(1)} fusion(bf16[3,100,64]{1,2,0:T(8,128)(2,1)S(1)} %copy-done, bf16[3,100,12500]{2,1,0:T(8,128)(2,1)} %param.13), kind=kOutput, calls=%fused_computation | convolution fusion | flops 480000000 | bytes 10738400 | tf_op jit(solution)/shard_map/dot_general | solution.py:38
  13.8 1.0 copy.25
  14.9 147.7 %all_to_all.4 = f32[8,8,12500]{2,0,1:T(8,128)S(1)} all-to-all(f32[8,8,12500]{2,0,1:T(8,128)S(1)} %copy.25), channel_id=1, replica_groups=mesh['opair'=4,'vpair'=8] {'vpair'}, dimensions={1} | all-to-all | bytes 6400000 | tf_op jit(solution)/shard_map/all_to_all | solution.py:42
  162.6 1.0 copy.26
  163.6 3.0 %reshape.160 = f32[8,100,1000]{2,1,0:T(8,128)} reshape(f32[8,8,12500]{2,1,0:T(8,128)S(1)} %copy.26) | data formatting | bytes 6400000 | tf_op jit(solution)/shard_map/reshape | solution.py:43
  166.6 0.0 copy-start.1
  166.6 5.3 %all-gather.2.cloned.1.call-done = bf16[800,3,1000]{2,1,0:T(4,128)(2,1)} async-done(((bf16[100,3,1000]{2,1,0:T(4,128)(2,1)}), bf16[800,3,1000]{2,1,0:T(4,128)(2,1)}) %all-gather.2.cloned.1.call-update) | async-done | bytes 4800016 | tf_op jit(solution)/shard_map/all_gather | solution.py:33
  171.9 11.5 %reshape.163 = bf16[8,100,3000]{2,1,0:T(8,128)(2,1)} reshape(bf16[800,3,1000]{2,1,0:T(4,128)(2,1)} %all-gather.2.cloned.1.call-done) | data formatting | bytes 9600000 | tf_op jit(solution)/shard_map/dot_general | solution.py:34
  183.3 0.0 copy-done.1
  183.3 0.0 copy-start.4
  183.3 0.0 copy-start.5
  183.3 0.0 copy-start.2
  183.4 0.0 copy-start.3
  183.4 10.3 %add_bitcast_fusion = f32[8,1,100,1000]{3,2,0,1:T(8,128)} fusion(f32[8,100,1000]{2,1,0:T(8,128)S(1)} %copy-done.1, bf16[8,100,3000]{2,1,0:T(8,128)(2,1)} %reshape.163, bf16[3000,1000,1]{1,0,2:T(8,128)(2,1)} %bitcast.24), kind=kOutput, calls=%fused_computation.1 | convolution fusion | flops 4800799744 | bytes 17200000 | tf_op jit(solution)/shard_map/dot_general | solution.py:34
  193.7 0.0 reduce-scatter.2.cloned.1.call-update
  195.0 0.0 copy-done.4
  195.0 0.2 reduce-window.6
  195.2 0.0 copy-done.5
  195.2 0.2 reduce-window.9
  195.4 0.0 copy-done.2
  195.4 0.6 dynamic_slice.7
  196.0 0.0 copy-done.3
  196.0 0.7 dynamic-slice_subtract_fusion
  196.7 0.6 fusion.1
  197.3 0.1 convert_reduce_fusion.1
  197.4 0.1 convert_reduce_fusion
  197.5 0.2 fusion
  197.7 0.7 broadcast_xor_fusion.1
  198.4 0.1 broadcast_add_fusion
  198.4 0.1 broadcast_xor_fusion
  198.5 32.5 %reduce-scatter.2.cloned.1.call-done = f32[2,1,100,1000]{3,2,0,1:T(8,128)} async-done(((f32[8,1,100,1000]{3,2,0,1:T(8,128)}), f32[2,1,100,1000]{3,2,0,1:T(8,128)}) %reduce-scatter.2.cloned.1.call-update) | async-done | bytes 800016 | tf_op jit(solution)/shard_map/reduce_scatter | solution.py:44
  231.0 1.5 divide_select_fusion
  232.5 1.7 copy.27
  (2 shorter events, 0.0 us)
Async XLA Ops:
  6.5 2.6 %copy-start = (bf16[3,100,64]{1,2,0:T(8,128)(2,1)S(1)}, bf16[3,100,64]{1,2,0:T(8,128)(2,1)}, u32[]{:S(2)}) copy-start(bf16[3,100,64]{1,2,0:T(8,128)(2,1)} %param.12) | copy-start | bytes 115204
  6.5 165.3 %all-gather.2.cloned.1.call-start = ((), (), s32[]{:S(2)}) async-start(), calls=%async_computation.2 | async-start | bytes 7372800 | tf_op jit(solution)/shard_map/all_gather | solution.py:33
  9.1 222.0 %reduce-scatter.2.cloned.1.call-start = ((), (), s32[]{:S(2)}) async-start(), calls=%async_computation.3 | async-start | bytes 4259840 | tf_op jit(solution)/shard_map/reduce_scatter | solution.py:44
  166.6 16.8 %copy-start.1 = (f32[8,100,1000]{2,1,0:T(8,128)S(1)}, f32[8,100,1000]{2,1,0:T(8,128)}, u32[]{:S(2)}) copy-start(f32[8,100,1000]{2,1,0:T(8,128)} %reshape.160) | copy-start | bytes 9600004
  183.3 11.7 %copy-start.4 = (s32[8]{0:T(128)S(1)}, s32[8]{0:T(128)}, u32[]{:S(2)}) copy-start(s32[8]{0:T(128)} %param.14) | copy-start | bytes 100
  183.3 11.9 %copy-start.5 = (s32[8]{0:T(128)S(1)}, s32[8]{0:T(128)}, u32[]{:S(2)}) copy-start(s32[8]{0:T(128)} %param.15) | copy-start | bytes 100
  183.3 12.0 %copy-start.2 = (f32[1000]{0:T(1024)S(1)}, f32[1000]{0:T(1024)}, u32[]{:S(2)}) copy-start(f32[1000]{0:T(1024)} %param.19) | copy-start | bytes 12004
  183.4 12.6 %copy-start.3 = (f32[100]{0:T(128)S(1)}, f32[100]{0:T(128)}, u32[]{:S(2)}) copy-start(f32[100]{0:T(128)} %param.18) | copy-start | bytes 1204
Sparse Core Ops, SparseCore 0:
  9.5 162.2 all-gather.1
  193.8 37.1 reduce-scatter.1
where the time goes:
time: 244 us; the launch traced here: 241 us
  blocking collectives  148 us (61%)
  waiting for transfers between devices  37.8 us (15%)
  local copies, waits for them, and re-layouts  21.4 us (9%)
  matrix products  15 us (6%)
  between operations  14.8 us (6%)
  other arithmetic  4.35 us (2%)
    all_to_all x1, blocking collectives, shards(): lax.all_to_all(cycle, 'vpair', split_axis=1, concat_axis=2, tiled=True)  148 us
    reduce_scatter x1, waiting for transfers between devices, shards(): resid = lax.psum_scatter(joined, 'opair', scatter_dimension=0, tiled=True)  32.5 us
    dot_general x1, local copies, waits for them, and re-layouts, shards(): jnp.dot(piece.reshape(piece.shape[0], slab_depth), ladder_flat, preferred...  11.5 us
    dot_general x1, matrix products, shards(): jnp.dot(piece.reshape(piece.shape[0], slab_depth), ladder_flat, preferred...  10.3 us
    all_gather x1, waiting for transfers between devices, shards(): piece = lax.all_gather(amplitudes, 'vpair', axis=0, tiled=True)  5.31 us
  transfers between devices with their start and end apart: 2, of which 2 were waited for; matrix products, arithmetic and copies ran while one was open for 5% of the time, Pallas kernels for 0%

commit v1 on v0

--- a/solution.py
+++ b/solution.py
@@ -1,12 +1,326 @@
+import functools
+
 import jax
 import jax.numpy as jnp
 from jax import lax
+from jax.experimental import pallas as pl
+from jax.experimental.pallas import tpu as pltpu
 from jax.sharding import PartitionSpec as P
 
 NO = 100
 NV = 1000
 I_DEV = 2
 A_DEV = 1
+NVP = 1024
+Q = 8
+FULL = 32000.0
+MESH = pl.DeviceIdType.MESH
+
+
+def up_to(n, m):
+    return (n + m - 1) // m * m
+
+
+def row_length(n_v):
+    x = 1
+    while (2 * x) * (2 * x) * 2 <= n_v and n_v % (2 * x) == 0:
+        x *= 2
+    return x
+
+
+def exponent(x):
+    top = jnp.max(jnp.max(jnp.abs(x), axis=1, keepdims=True), axis=0, keepdims=True)
+    return jnp.floor(jnp.log(jnp.maximum(top, 1e-30)) * 1.4426950408889634) + 1.0
+
+
+def code(x, e, is_scale):
+    q = jnp.round(x * (FULL * jnp.exp2(-e)))
+    return jnp.where(is_scale, e, q).astype(jnp.int32).astype(jnp.int16)
+
+
+def decode(q, e):
+    return q.astype(jnp.float32) * (jnp.exp2(e) * (1.0 / FULL))
+
+
+def kernel(
+    n_o, n_v, pairs, pairs_pad, depth, jb, jb_pad, ch, a_win,
+    amps, ints, w_ref, cyc_ints, lad_out, cyc_out,
+    gat, b_buf, y_buf, part, cs, cr, total, tile, asend, arecv, acc, ls, lr,
+    copy_sem, a_recv, up_send, down_send, x_send, c_send, c_recv, t_send, t_recv, l_send, l_recv,
+):
+    o = lax.axis_index("opair")
+    v = lax.axis_index("vpair")
+    nx = row_length(n_v)
+    nz = n_v // nx
+    z, x = v // nx, v % nx
+    rows = a_win * I_DEV
+    per_owner = n_v // n_o
+
+    b_copy = pltpu.make_async_copy(ints, b_buf, copy_sem.at[0])
+    y_copy = pltpu.make_async_copy(cyc_ints, y_buf, copy_sem.at[1])
+    own_copy = pltpu.make_async_copy(amps, gat.at[v], copy_sem.at[2])
+    y_copy.start()
+    own_copy.start()
+    b_copy.start()
+
+    barrier = pltpu.get_barrier_semaphore()
+    for t in range(1, n_v):
+        pl.semaphore_signal(barrier, inc=1, device_id=(o, (v + t) % n_v), device_id_type=MESH)
+    for s in range(1, n_o):
+        pl.semaphore_signal(barrier, inc=1, device_id=((o + s) % n_o, v), device_id_type=MESH)
+    pl.semaphore_wait(barrier, n_v - 1 + n_o - 1)
+
+    def hop(src, slot, c, send, to):
+        return pltpu.make_async_remote_copy(
+            src_ref=src, dst_ref=gat.at[slot, c], send_sem=send, recv_sem=a_recv.at[slot, c],
+            device_id=(o, to), device_id_type=MESH,
+        )
+
+    def block_src(slot, c, own):
+        return amps.at[c] if own else gat.at[slot, c]
+
+    def up_hop(d, c):
+        slot = (z - d) * nx + x
+        return hop(block_src(slot, c, d == 0), slot, c, up_send.at[d, c], v + nx)
+
+    def down_hop(d, c):
+        slot = (z + d) * nx + x
+        return hop(block_src(slot, c, d == 0), slot, c, down_send.at[d, c], v - nx)
+
+    def x_hops(k, zb, c):
+        slot = zb * nx + x
+        return [
+            hop(block_src(slot, c, k == 0), slot, c, x_send.at[k, t - 1, c], z * nx + (x + t) % nx)
+            for t in range(1, nx)
+        ]
+
+    def arrived(slot, c):
+        pltpu.make_async_remote_copy(
+            src_ref=gat.at[slot, c], dst_ref=gat.at[slot, c], send_sem=copy_sem.at[0],
+            recv_sem=a_recv.at[slot, c], device_id=(o, v), device_id_type=MESH,
+        ).wait_recv()
+
+    for c in range(depth):
+        if nz > 1:
+            @pl.when(z + 1 < nz)
+            def _():
+                up_hop(0, c).start()
+
+            @pl.when(z >= 1)
+            def _():
+                down_hop(0, c).start()
+        for h in x_hops(0, z, c):
+            h.start()
+
+    acc[...] = jnp.zeros_like(acc)
+    part[:, jb_pad - 128:] = jnp.zeros((part.shape[0], 128), jnp.float32)
+    y_copy.wait()
+    step = 14 * 128
+    for at in range(0, jb, step):
+        end = min(at + step, jb)
+        sum_c = None
+        for c in range(depth):
+            term = jnp.dot(w_ref[c], y_buf[c, :, at:end], preferred_element_type=jnp.float32)
+            sum_c = term if sum_c is None else sum_c + term
+        part[:, at:end] = sum_c
+
+    is_scale_c = lax.broadcasted_iota(jnp.int32, (rows, jb_pad), 1) == jb_pad - 1
+
+    def c_hop(s):
+        return pltpu.make_async_remote_copy(
+            src_ref=cs.at[s - 1], dst_ref=cr.at[s - 1], send_sem=c_send.at[s - 1],
+            recv_sem=c_recv.at[s - 1], device_id=((o + s) % n_o, v), device_id_type=MESH,
+        )
+
+    for s in range(1, n_o):
+        to = (o + s) % n_o
+        block = part[pl.ds(pl.multiple_of(to * rows, rows), rows), :]
+        cs[s - 1] = code(block, exponent(block), is_scale_c)
+        c_hop(s).start()
+
+    col = lax.broadcasted_iota(jnp.int32, (pairs_pad, NVP), 1)
+
+    def l_hop(slot):
+        owner = slot // per_owner
+        return pltpu.make_async_remote_copy(
+            src_ref=ls.at[slot], dst_ref=lr.at[o, slot % per_owner], send_sem=l_send.at[slot],
+            recv_sem=l_recv.at[o, slot % per_owner], device_id=(owner, v), device_id_type=MESH,
+        )
+
+    def multiply(slot):
+        for at in range(0, NV, 256):
+            end = min(at + 256, NV)
+            sum_c = None
+            for c in range(depth):
+                term = jnp.dot(gat[slot, c], b_buf[c, :, at:end], preferred_element_type=jnp.float32)
+                sum_c = term if sum_c is None else sum_c + term
+            acc[:, at:end] = sum_c
+
+        @pl.when(slot // per_owner == o)
+        def _():
+            lad_out[slot % per_owner] = acc[...]
+
+        @pl.when(slot // per_owner != o)
+        def _():
+            block = acc[...]
+            ls[slot] = code(block, exponent(block), col >= NV)
+            l_hop(slot).start()
+
+    def take_row(zb):
+        def one(t, _):
+            slot = zb * nx + (x + t) % nx
+            for c in range(depth):
+                arrived(slot, c)
+            multiply(slot)
+            return 0
+
+        lax.fori_loop(1, nx, one, 0)
+
+    own_copy.wait()
+    b_copy.wait()
+    multiply(v)
+
+    def t_hop(t):
+        to = (v + t) % n_v
+        return pltpu.make_async_remote_copy(
+            src_ref=asend.at[to], dst_ref=arecv.at[v], send_sem=t_send.at[t - 1],
+            recv_sem=t_recv.at[t - 1], device_id=(o, to), device_id_type=MESH,
+        )
+
+    def cycle_exchange():
+        sum_o = part[pl.ds(pl.multiple_of(o * rows, rows), rows), :]
+        for s in range(1, n_o):
+            c_hop(s).wait_recv()
+            got = cr[s - 1]
+            e = got[rows - 1:rows, jb_pad - 128:].astype(jnp.float32)[:, 127:128]
+            sum_o = sum_o + jnp.where(is_scale_c, 0.0, decode(got, e))
+        total[:, 0:jb_pad] = sum_o
+        total[:, jb_pad:] = jnp.zeros((rows, Q * ch - jb_pad), jnp.float32)
+        spot = (lax.broadcasted_iota(jnp.int32, (I_DEV * Q, ch), 0) == I_DEV * Q - 1) & (
+            lax.broadcasted_iota(jnp.int32, (I_DEV * Q, ch), 1) == ch - 1
+        )
+
+        def one(t, _):
+            a = (v + t) % n_v
+            for i in range(I_DEV):
+                for q in range(Q):
+                    tile[a, i * Q + q:i * Q + q + 1, :] = total[pl.ds(a * I_DEV + i, 1), q * ch:q * ch + ch]
+            block = tile[a]
+            asend[a] = code(block, exponent(block), spot)
+            return 0
+
+        lax.fori_loop(0, n_v, one, 0)
+        for t in range(1, n_v):
+            t_hop(t).start()
+
+    for d in range(1, nz):
+        for c in range(depth):
+            @pl.when(z - d >= 0)
+            def _():
+                arrived((z - d) * nx + x, c)
+
+                @pl.when(z + 1 < nz)
+                def _():
+                    up_hop(d, c).start()
+
+                for h in x_hops(d, z - d, c):
+                    h.start()
+
+            @pl.when(z + d < nz)
+            def _():
+                arrived((z + d) * nx + x, c)
+
+                @pl.when(z >= 1)
+                def _():
+                    down_hop(d, c).start()
+
+                for h in x_hops(nz - 1 + d, z + d, c):
+                    h.start()
+
+        if d == min(2, nz - 1):
+            cycle_exchange()
+        if d == 1:
+            take_row(z)
+        else:
+            @pl.when(z - (d - 1) >= 0)
+            def _():
+                take_row(z - (d - 1))
+
+            @pl.when(z + (d - 1) < nz)
+            def _():
+                take_row(z + (d - 1))
+
+        @pl.when(z - d >= 0)
+        def _():
+            multiply((z - d) * nx + x)
+
+        @pl.when(z + d < nz)
+        def _():
+            multiply((z + d) * nx + x)
+
+    @pl.when(z - (nz - 1) >= 0)
+    def _():
+        take_row(z - (nz - 1))
+
+    @pl.when(z + (nz - 1) < nz)
+    def _():
+        take_row(z + (nz - 1))
+
+    cyc_out[v] = tile[v]
+    for t in range(1, n_v):
+        t_hop(t).wait_recv()
+        src = (v + n_v - t) % n_v
+        got = arecv[src]
+        e = got[:, ch - 128:].astype(jnp.float32)[I_DEV * Q - 1:I_DEV * Q, 127:128]
+        cyc_out[src] = decode(got, e)
+
+    for s in range(1, n_o):
+        src = (o + s) % n_o
+        for b in range(per_owner):
+            pltpu.make_async_remote_copy(
+                src_ref=ls.at[0], dst_ref=lr.at[src, b], send_sem=l_send.at[0],
+                recv_sem=l_recv.at[src, b], device_id=(o, v), device_id_type=MESH,
+            ).wait_recv()
+            got = lr[src, b]
+            e = got[:, NVP - 128:].astype(jnp.float32)[0:1, 127:128]
+            lad_out[b] = lad_out[b] + decode(got, e)
+
+    for d in range(nz):
+        for c in range(depth):
+            if d < nz - 1:
+                @pl.when((z - d >= 0) & (z + 1 < nz))
+                def _():
+                    up_hop(d, c).wait_send()
+
+                @pl.when((z + d < nz) & (z >= 1))
+                def _():
+                    down_hop(d, c).wait_send()
+            if d == 0:
+                for h in x_hops(0, z, c):
+                    h.wait_send()
+            else:
+                @pl.when(z - d >= 0)
+                def _():
+                    for h in x_hops(d, z - d, c):
+                        h.wait_send()
+
+                @pl.when(z + d < nz)
+                def _():
+                    for h in x_hops(nz - 1 + d, z + d, c):
+                        h.wait_send()
+    for s in range(1, n_o):
+        c_hop(s).wait_send()
+    for t in range(1, n_v):
+        t_hop(t).wait_send()
+
+    def sent(slot, _):
+        @pl.when(slot // per_owner != o)
+        def _():
+            l_hop(slot).wait_send()
+
+        return 0
+
+    lax.fori_loop(0, n_v, sent, 0)
 
 
 def irrep_of(blocks, index):
@@ -26,22 +340,73 @@
     eps_occ,
     eps_virt,
 ):
-    i_win = I_DEV * lax.axis_size("opair")
-    a_win = A_DEV * lax.axis_size("vpair")
-    slab_depth = ladder_ints.shape[0] * ladder_ints.shape[1]
-    ladder_flat = ladder_ints.reshape(slab_depth, A_DEV * NV)
-    piece = lax.all_gather(amplitudes, "vpair", axis=0, tiled=True)
-    ladder = jnp.dot(
-        piece.reshape(piece.shape[0], slab_depth), ladder_flat, preferred_element_type=jnp.float32
-    )
-    ladder = ladder.reshape(i_win, NO, A_DEV, NV).transpose(0, 2, 1, 3)
-    cycle = lax.dot_general(
-        cycle_amps, cycle_ints, (((0, 1), (0, 1)), ((), ())), preferred_element_type=jnp.float32
-    )
-    cycle = cycle.reshape(i_win, a_win, cycle_ints.shape[2])
-    moved = lax.all_to_all(cycle, "vpair", split_axis=1, concat_axis=2, tiled=True)
-    joined = ladder + moved.reshape(i_win, A_DEV, NO, NV)
-    resid = lax.psum_scatter(joined, "opair", scatter_dimension=0, tiled=True)
+    n_o, n_v = lax.axis_size("opair"), lax.axis_size("vpair")
+    a_win = A_DEV * n_v
+    pairs, depth = amplitudes.shape[:2]
+    pairs_pad = up_to(pairs, 16)
+    jb = cycle_ints.shape[2]
+    jb_pad = up_to(jb + 1, 128)
+    ch = up_to((jb_pad + Q) // Q, 128)
+    rows = a_win * I_DEV
+    per_owner = n_v // n_o
+    nx = row_length(n_v)
+    nz = n_v // nx
+
+    amps = jnp.pad(amplitudes.transpose(1, 0, 2), ((0, 0), (0, pairs_pad - pairs), (0, 0)))
+    ints = ladder_ints.reshape(depth, NV, NV)
+    w = cycle_amps.reshape(depth, NO, n_o, I_DEV, a_win).transpose(0, 2, 4, 3, 1).reshape(depth, n_o * rows, NO)
+    dma = pltpu.SemaphoreType.DMA
+    lad, cyc = pl.pallas_call(
+        functools.partial(kernel, n_o, n_v, pairs, pairs_pad, depth, jb, jb_pad, ch, a_win),
+        out_shape=(
+            jax.ShapeDtypeStruct((per_owner, pairs_pad, NVP), jnp.float32),
+            jax.ShapeDtypeStruct((n_v, I_DEV * Q, ch), jnp.float32),
+        ),
+        in_specs=[
+            pl.BlockSpec(memory_space=pl.ANY),
+            pl.BlockSpec(memory_space=pl.ANY),
+            pl.BlockSpec(memory_space=pltpu.VMEM),
+            pl.BlockSpec(memory_space=pl.ANY),
+        ],
+        out_specs=[pl.BlockSpec(memory_space=pltpu.VMEM)] * 2,
+        scratch_shapes=[
+            pltpu.VMEM((n_v, depth, pairs_pad, NV), jnp.bfloat16),
+            pltpu.VMEM((depth, NV, NV), jnp.bfloat16),
+            pltpu.VMEM((depth, NO, jb), jnp.bfloat16),
+            pltpu.VMEM((n_o * rows, jb_pad), jnp.float32),
+            pltpu.VMEM((n_o - 1, rows, jb_pad), jnp.int16),
+            pltpu.VMEM((n_o - 1, rows, jb_pad), jnp.int16),
+            pltpu.VMEM((rows, Q * ch), jnp.float32),
+            pltpu.VMEM((n_v, I_DEV * Q, ch), jnp.float32),
+            pltpu.VMEM((n_v, I_DEV * Q, ch), jnp.int16),
+            pltpu.VMEM((n_v, I_DEV * Q, ch), jnp.int16),
+            pltpu.VMEM((pairs_pad, NVP), jnp.float32),
+            pltpu.VMEM((n_v, pairs_pad, NVP), jnp.int16),
+            pltpu.VMEM((n_o, per_owner, pairs_pad, NVP), jnp.int16),
+            dma((3,)),
+            dma((n_v, depth)),
+            dma((nz, depth)),
+            dma((nz, depth)),
+            dma((2 * nz - 1, max(nx - 1, 1), depth)),
+            dma((n_o - 1,)),
+            dma((n_o - 1,)),
+            dma((n_v - 1,)),
+            dma((n_v - 1,)),
+            dma((n_v,)),
+            dma((n_o, per_owner)),
+        ],
+        compiler_params=pltpu.CompilerParams(
+            collective_id=0, has_side_effects=True, vmem_limit_bytes=58 * 1024 * 1024
+        ),
+        cost_estimate=pl.CostEstimate(
+            flops=2 * n_v * pairs * depth * NV * NV + 2 * n_o * rows * depth * NO * jb,
+            bytes_accessed=2 * depth * (NV * NV + NO * jb), transcendentals=0,
+        ),
+        name="residual",
+    )(amps, ints, w, cycle_ints)
+    ladder = lad[:, :pairs, :NV].reshape(I_DEV, A_DEV, NO, NV)
+    cycle = cyc.reshape(n_v, I_DEV, Q * ch)[:, :, :jb].transpose(1, 0, 2).reshape(I_DEV, A_DEV, NO, NV)
+    resid = ladder + cycle
     first_occ = occ_start[0] + lax.axis_index("opair") * I_DEV
     first_virt = virt_start[0] + lax.axis_index("vpair") * A_DEV
     glob_i = first_occ + jnp.arange(I_DEV, dtype=jnp.int32)

time: 244 us -> 94.3 us (0.39)
  blocking collectives: 148 us -> 0 us
  Pallas kernels: 0 us -> 79.9 us
  waiting for transfers between devices: 37.8 us -> 0 us
  matrix products: 15 us -> 0 us
  between operations: 14.8 us -> 1.41 us
  local copies, waits for them, and re-layouts: 21.4 us -> 8.02 us
    all_to_all x1 -> x0, blocking collectives: 148 us -> none  [shards(): lax.all_to_all(cycle, 'vpair', split_axis=1, concat_axis=2, tiled=True)]
    pallas_call x0 -> x1, Pallas kernels: none -> 79.9 us  [shards(): pl.pallas_call(functools.partial(kernel, n_o, n_v, pairs, pairs_pad, dept...]
    reduce_scatter x1 -> x0, waiting for transfers between devices: 32.5 us -> none  [shards(): resid = lax.psum_scatter(joined, 'opair', scatter_dimension=0, tiled=True)]
    dot_general x2 -> x0, matrix products: 15 us -> none  [the longest x1 10.3 us: shards(): jnp.dot(piece.reshape(piece.shape[0], slab_depth), ladder_flat, preferred...]
    dot_general x1 -> x0, local copies, waits for them, and re-layouts: 11.5 us -> none  [shards(): jnp.dot(piece.reshape(piece.shape[0], slab_depth), ladder_flat, preferred...]
    all_gather x1 -> x0, waiting for transfers between devices: 5.31 us -> none  [shards(): piece = lax.all_gather(amplitudes, 'vpair', axis=0, tiled=True)]
    unnamed x13 -> x9, local copies, waits for them, and re-layouts: 2.54 us -> 0.07 us
  transfers between devices with their start and end apart: 2 -> 0, of which waited for: 2 -> 0; matrix products, arithmetic and copies ran while one was open for 5% -> 0% of each run, Pallas kernels for 0% -> 0%
where the time goes in v1:
time: 94.3 us; the launch traced here: 93.7 us
  Pallas kernels  79.9 us (85%)
  local copies, waits for them, and re-layouts  8.02 us (9%)
  other arithmetic  4.41 us (5%)
  between operations  1.41 us (1%)
    pallas_call x1, Pallas kernels, shards(): pl.pallas_call(functools.partial(kernel, n_o, n_v, pairs, pairs_pad, dept...  79.9 us
    reshape x2, local copies, waits for them, and re-layouts, shards(): cyc.reshape(n_v, I_DEV, Q * ch)[:, :, :jb].transpose(1, 0, 2)  2.11 us
    pad x1, local copies, waits for them, and re-layouts, shards(): jnp.pad(amplitudes.transpose(1, 0, 2), ((0, 0), (0, pairs_pad - pairs), (...  2.01 us

profile of v1, /device:TPU:5, one launch (start us, length us, event | category | flops | bytes accessed | tf_op | source)
XLA Modules:
  0.0 93.7 jit_solution(15557565440769984522)
XLA Ops:
  0.0 2.0 %pad.4.amps = bf16[3,112,1000]{2,1,0:T(8,128)(2,1)} pad(bf16[3,100,1000]{2,1,0:T(8,128)(2,1)} %bitcast.23, bf16[]{:T(256)} %constant.23.clone.1), padding=0_0x0_12x0_0 | pad | bytes 1272002 | tf_op jit(solution)/shard_map/jit(_pad)/pad | solution.py:355
  2.0 1.5 %copy.17 = bf16[3,100,4,2,8]{1,3,4,2,0:T(2,128)(2,1)} copy(bf16[3,100,4,2,8]{1,4,3,2,0:T(8,128)(2,1)} %bitcast.24) | data formatting | bytes 76800 | tf_op jit(solution)/shard_map/reshape | solution.py:357
  3.5 0.0 copy-start
  3.5 0.0 copy-start.1
  3.5 0.0 copy-start.2
  3.5 0.0 copy-start.3
  3.5 79.9 %residual.1 = (f32[2,112,1024]{2,1,0:T(8,128)}, f32[8,16,1664]{2,1,0:T(8,128)}) custom-call(bf16[3,112,1000]{2,1,0:T(8,128)(2,1)} %pad.4.amps, bf16[3,1000,1000]{2,1,0:T(8,128)(2,1)} %bitcast.26, bf16[3,64,100]{2,1,0:T(8,128)(2,1)} %bitcast.25, bf16[3,100,12500]{2,1,0:T(8,128)(2,1)} %cyc_ints.1), custom_call_target="tpu_custom_call" | custom-call | flops 5280000000 | bytes 13500000 | tf_op jit(solution)/shard_map/residual/pallas_call | solution.py:359
  83.4 1.7 %reshape.153 = f32[8,2,13312]{2,1,0:T(2,128)S(1)} reshape(f32[8,16,1664]{2,1,0:T(8,128)} %get-tuple-element.8) | data formatting | bytes 1703936 | tf_op jit(solution)/shard_map/reshape | solution.py:408
  85.0 0.1 slice.20
  85.1 0.1 copy.22
  85.2 0.4 reshape.154
  86.9 0.0 copy-done
  86.9 0.6 dynamic_slice.7
  87.5 0.0 copy-done.1
  87.5 0.7 dynamic-slice_subtract_fusion
  88.3 0.1 broadcast_add_fusion
  88.3 0.0 copy-done.2
  88.3 0.2 reduce-window.9
  88.5 0.6 fusion.1
  89.1 0.1 convert_reduce_fusion
  89.2 0.0 copy-done.3
  89.2 0.2 reduce-window.6
  89.4 0.1 convert_reduce_fusion.1
  89.5 0.1 broadcast_xor_fusion
  89.6 0.2 fusion
  89.8 0.6 broadcast_xor_fusion.1
  90.5 1.5 %select_bitcast_fusion = f32[2,1,100,1000]{3,2,0,1:T(8,128)S(1)} fusion(f32[2,100,1000]{2,1,0:T(8,128)S(1)} %reshape.154, f32[2,112,1024]{2,1,0:T(8,128)} %get-tuple-element.7, f32[1000]{0:T(1024)S(1)} %copy-done, f32[2,100]{1,0:T(2,128)S(1)} %broadcast_add_fusion, s32[100,1000]{1,0:T(8,128)S(1)} %broadcast_xor_fusion, s32[2]{0:T(128)S(1)} %broadcast_xor_fusion.1), kind=kLoop, calls=%fused_computation | loop fusion | flops 1200000 | bytes 2804808 | tf_op jit(solution)/shard_map/jit(_where)/select_n | solution.py:430
  92.0 1.7 %copy.19 = f32[2,1,100,1000]{3,1,2,0:T(1,128)} copy(f32[2,1,100,1000]{3,2,0,1:T(8,128)S(1)} %select_bitcast_fusion) | data formatting | bytes 1600000 | tf_op jit(solution)/shard_map/jit(_where)/select_n | solution.py:430
  (2 shorter events, 0.0 us)
Async XLA Ops:
  3.5 83.5 %copy-start = (f32[1000]{0:T(1024)S(1)}, f32[1000]{0:T(1024)}, u32[]{:S(2)}) copy-start(f32[1000]{0:T(1024)} %param.19) | copy-start | bytes 12004
  3.5 84.1 %copy-start.1 = (f32[100]{0:T(128)S(1)}, f32[100]{0:T(128)}, u32[]{:S(2)}) copy-start(f32[100]{0:T(128)} %param.18) | copy-start | bytes 1204
  3.5 84.9 %copy-start.2 = (s32[8]{0:T(128)S(1)}, s32[8]{0:T(128)}, u32[]{:S(2)}) copy-start(s32[8]{0:T(128)} %param.15) | copy-start | bytes 100
  3.5 85.8 %copy-start.3 = (s32[8]{0:T(128)S(1)}, s32[8]{0:T(128)}, u32[]{:S(2)}) copy-start(s32[8]{0:T(128)} %param.14) | copy-start | bytes 100

commit v2 on v1

--- a/solution.py
+++ b/solution.py
@@ -45,8 +45,8 @@
 def kernel(
     n_o, n_v, pairs, pairs_pad, depth, jb, jb_pad, ch, a_win,
     amps, ints, w_ref, cyc_ints, lad_out, cyc_out,
-    gat, b_buf, y_buf, part, cs, cr, total, tile, asend, arecv, acc, ls, lr,
-    copy_sem, a_recv, up_send, down_send, x_send, c_send, c_recv, t_send, t_recv, l_send, l_recv,
+    a_buf, gat, rest, rest_sum, b_buf, y_buf, part, cs, cr, total, tile, asend, arecv, acc, ls, lr,
+    copy_sem, a_recv, up_send, down_send, x_send, cross_send, c_send, c_recv, t_send, t_recv, l_send, l_recv,
 ):
     o = lax.axis_index("opair")
     v = lax.axis_index("vpair")
@@ -55,12 +55,15 @@
     z, x = v // nx, v % nx
     rows = a_win * I_DEV
     per_owner = n_v // n_o
+    base = pairs // 16 * 16
+    left = pairs - base
+    pieces = depth + 1
 
     b_copy = pltpu.make_async_copy(ints, b_buf, copy_sem.at[0])
     y_copy = pltpu.make_async_copy(cyc_ints, y_buf, copy_sem.at[1])
-    own_copy = pltpu.make_async_copy(amps, gat.at[v], copy_sem.at[2])
+    own_copy = pltpu.make_async_copy(amps, a_buf, copy_sem.at[2])
+    own_copy.start()
     y_copy.start()
-    own_copy.start()
     b_copy.start()
 
     barrier = pltpu.get_barrier_semaphore()
@@ -68,16 +71,24 @@
         pl.semaphore_signal(barrier, inc=1, device_id=(o, (v + t) % n_v), device_id_type=MESH)
     for s in range(1, n_o):
         pl.semaphore_signal(barrier, inc=1, device_id=((o + s) % n_o, v), device_id_type=MESH)
+    rest_sum[...] = jnp.zeros_like(rest_sum)
+    own_copy.wait()
+    for c in range(depth):
+        rest_sum[0, c * left:(c + 1) * left, 0:NV] = a_buf[c, base:pairs, :].astype(jnp.float32)
+    rest[v] = rest_sum[0, :, 0:NV].astype(jnp.bfloat16)
     pl.semaphore_wait(barrier, n_v - 1 + n_o - 1)
+
+    def piece(slot, c):
+        return gat.at[slot, c] if c < depth else rest.at[slot]
 
     def hop(src, slot, c, send, to):
         return pltpu.make_async_remote_copy(
-            src_ref=src, dst_ref=gat.at[slot, c], send_sem=send, recv_sem=a_recv.at[slot, c],
+            src_ref=src, dst_ref=piece(slot, c), send_sem=send, recv_sem=a_recv.at[slot, c],
             device_id=(o, to), device_id_type=MESH,
         )
 
     def block_src(slot, c, own):
-        return amps.at[c] if own else gat.at[slot, c]
+        return a_buf.at[c, pl.ds(0, base)] if own and c < depth else piece(slot, c)
 
     def up_hop(d, c):
         slot = (z - d) * nx + x
@@ -88,19 +99,26 @@
         return hop(block_src(slot, c, d == 0), slot, c, down_send.at[d, c], v - nx)
 
     def x_hops(k, zb, c):
+        if (k == 1 or k == nz) and c == depth - 1:
+            return []
         slot = zb * nx + x
         return [
             hop(block_src(slot, c, k == 0), slot, c, x_send.at[k, t - 1, c], z * nx + (x + t) % nx)
             for t in range(1, nx)
         ]
 
+    def cross(k, t):
+        slot = z * nx + (x + t) % nx
+        c = depth - 1
+        return hop(gat.at[slot, c], slot, c, cross_send.at[k, t - 1], v + nx if k == 0 else v - nx)
+
     def arrived(slot, c):
         pltpu.make_async_remote_copy(
-            src_ref=gat.at[slot, c], dst_ref=gat.at[slot, c], send_sem=copy_sem.at[0],
+            src_ref=piece(slot, c), dst_ref=piece(slot, c), send_sem=copy_sem.at[0],
             recv_sem=a_recv.at[slot, c], device_id=(o, v), device_id_type=MESH,
         ).wait_recv()
 
-    for c in range(depth):
+    for c in range(pieces):
         if nz > 1:
             @pl.when(z + 1 < nz)
             def _():
@@ -152,9 +170,15 @@
             end = min(at + 256, NV)
             sum_c = None
             for c in range(depth):
-                term = jnp.dot(gat[slot, c], b_buf[c, :, at:end], preferred_element_type=jnp.float32)
-                sum_c = term if sum_c is None else sum_c + term
-            acc[:, at:end] = sum_c
+                lhs = jnp.concatenate([gat[slot, c], rest[slot]], axis=0)
+                term = jnp.dot(lhs, b_buf[c, :, at:end], preferred_element_type=jnp.float32)
+                rest_sum[c, :, at:end] = term[base:]
+                sum_c = term[:base] if sum_c is None else sum_c + term[:base]
+            acc[0:base, at:end] = sum_c
+        end_sum = rest_sum[0, 0:left, :]
+        for c in range(1, depth):
+            end_sum = end_sum + rest_sum[c, c * left:(c + 1) * left, :]
+        acc[base:pairs, :] = end_sum
 
         @pl.when(slot // per_owner == o)
         def _():
@@ -169,15 +193,16 @@
     def take_row(zb):
         def one(t, _):
             slot = zb * nx + (x + t) % nx
-            for c in range(depth):
+            for c in range(pieces):
                 arrived(slot, c)
             multiply(slot)
             return 0
 
         lax.fori_loop(1, nx, one, 0)
 
-    own_copy.wait()
     b_copy.wait()
+    for c in range(depth):
+        gat[v, c] = a_buf[c, 0:base, :]
     multiply(v)
 
     def t_hop(t):
@@ -204,7 +229,7 @@
             a = (v + t) % n_v
             for i in range(I_DEV):
                 for q in range(Q):
-                    tile[a, i * Q + q:i * Q + q + 1, :] = total[pl.ds(a * I_DEV + i, 1), q * ch:q * ch + ch]
+                    tile[a, i * Q + q:i * Q + q + 1, :] = total[pl.ds(i * a_win + a, 1), q * ch:q * ch + ch]
             block = tile[a]
             asend[a] = code(block, exponent(block), spot)
             return 0
@@ -214,7 +239,7 @@
             t_hop(t).start()
 
     for d in range(1, nz):
-        for c in range(depth):
+        for c in range(pieces):
             @pl.when(z - d >= 0)
             def _():
                 arrived((z - d) * nx + x, c)
@@ -240,7 +265,26 @@
         if d == min(2, nz - 1):
             cycle_exchange()
         if d == 1:
-            take_row(z)
+            for t in range(1, nx):
+                arrived(z * nx + (x + t) % nx, depth - 1)
+
+                @pl.when(z + 1 < nz)
+                def _():
+                    cross(0, t).start()
+
+                @pl.when(z >= 1)
+                def _():
+                    cross(1, t).start()
+
+            def one(t, _):
+                slot = z * nx + (x + t) % nx
+                for c in range(pieces):
+                    if c != depth - 1:
+                        arrived(slot, c)
+                multiply(slot)
+                return 0
+
+            lax.fori_loop(1, nx, one, 0)
         else:
             @pl.when(z - (d - 1) >= 0)
             def _():
@@ -286,7 +330,7 @@
             lad_out[b] = lad_out[b] + decode(got, e)
 
     for d in range(nz):
-        for c in range(depth):
+        for c in range(pieces):
             if d < nz - 1:
                 @pl.when((z - d >= 0) & (z + 1 < nz))
                 def _():
@@ -308,6 +352,15 @@
                 def _():
                     for h in x_hops(nz - 1 + d, z + d, c):
                         h.wait_send()
+    for t in range(1, nx):
+        @pl.when(z + 1 < nz)
+        def _():
+            cross(0, t).wait_send()
+
+        @pl.when(z >= 1)
+        def _():
+            cross(1, t).wait_send()
+
     for s in range(1, n_o):
         c_hop(s).wait_send()
     for t in range(1, n_v):
@@ -352,9 +405,11 @@
     nx = row_length(n_v)
     nz = n_v // nx
 
-    amps = jnp.pad(amplitudes.transpose(1, 0, 2), ((0, 0), (0, pairs_pad - pairs), (0, 0)))
+    amps = amplitudes.transpose(1, 0, 2)
+    base = pairs // 16 * 16
+    short = up_to(depth * (pairs - base), 16)
     ints = ladder_ints.reshape(depth, NV, NV)
-    w = cycle_amps.reshape(depth, NO, n_o, I_DEV, a_win).transpose(0, 2, 4, 3, 1).reshape(depth, n_o * rows, NO)
+    w = cycle_amps.transpose(0, 2, 1)
     dma = pltpu.SemaphoreType.DMA
     lad, cyc = pl.pallas_call(
         functools.partial(kernel, n_o, n_v, pairs, pairs_pad, depth, jb, jb_pad, ch, a_win),
@@ -370,7 +425,10 @@
         ],
         out_specs=[pl.BlockSpec(memory_space=pltpu.VMEM)] * 2,
         scratch_shapes=[
-            pltpu.VMEM((n_v, depth, pairs_pad, NV), jnp.bfloat16),
+            pltpu.VMEM((depth, pairs, NV), jnp.bfloat16),
+            pltpu.VMEM((n_v, depth, base, NV), jnp.bfloat16),
+            pltpu.VMEM((n_v, short, NV), jnp.bfloat16),
+            pltpu.VMEM((depth, short, NVP), jnp.float32),
             pltpu.VMEM((depth, NV, NV), jnp.bfloat16),
             pltpu.VMEM((depth, NO, jb), jnp.bfloat16),
             pltpu.VMEM((n_o * rows, jb_pad), jnp.float32),
@@ -384,10 +442,11 @@
             pltpu.VMEM((n_v, pairs_pad, NVP), jnp.int16),
             pltpu.VMEM((n_o, per_owner, pairs_pad, NVP), jnp.int16),
             dma((3,)),
-            dma((n_v, depth)),
-            dma((nz, depth)),
-            dma((nz, depth)),
-            dma((2 * nz - 1, max(nx - 1, 1), depth)),
+            dma((n_v, depth + 1)),
+            dma((nz, depth + 1)),
+            dma((nz, depth + 1)),
+            dma((2 * nz - 1, max(nx - 1, 1), depth + 1)),
+            dma((2, max(nx - 1, 1))),
             dma((n_o - 1,)),
             dma((n_o - 1,)),
             dma((n_v - 1,)),

time: 94.3 us -> 85.6 us (0.908)
  Pallas kernels: 79.9 us -> 74.9 us
  local copies, waits for them, and re-layouts: 8.02 us -> 4.56 us
    pallas_call x1, Pallas kernels: 79.9 us -> 74.9 us  [shards(): pl.pallas_call(functools.partial(kernel, n_o, n_v, pairs, pairs_pad, dept...]
    pad x1 -> x0, local copies, waits for them, and re-layouts: 2.01 us -> none  [shards(): jnp.pad(amplitudes.transpose(1, 0, 2), ((0, 0), (0, pairs_pad - pairs), (...]
    reshape x1 -> x0, local copies, waits for them, and re-layouts: 1.45 us -> none  [shards(): cycle_amps.reshape(depth, NO, n_o, I_DEV, a_win).transpose(0, 2, 4, 3, 1)]
where the time goes in v2:
time: 85.6 us; the launch traced here: 85.3 us
  Pallas kernels  74.9 us (88%)
  local copies, waits for them, and re-layouts  4.56 us (5%)
  other arithmetic  4.41 us (5%)
  between operations  1.42 us (2%)
    pallas_call x1, Pallas kernels, shards(): pl.pallas_call(functools.partial(kernel, n_o, n_v, pairs, pairs_pad, dept...  74.9 us
    reshape x2, local copies, waits for them, and re-layouts, shards(): cyc.reshape(n_v, I_DEV, Q * ch)[:, :, :jb].transpose(1, 0, 2)  2.11 us
    select_n x1, local copies, waits for them, and re-layouts, shards(): return jnp.where(total_sym == 0, resid / denom, jnp.float32(0.0))  1.73 us

profile of v2, /device:TPU:5, one launch (start us, length us, event | category | flops | bytes accessed | tf_op | source)
XLA Modules:
  0.0 85.3 jit_solution(10462341515438800585)
XLA Ops:
  0.0 0.0 copy-start
  0.0 0.0 copy-start.1
  0.0 0.0 copy-start.2
  0.0 0.0 copy-start.3
  0.0 74.9 %residual.1 = (f32[2,112,1024]{2,1,0:T(8,128)}, f32[8,16,1664]{2,1,0:T(8,128)}) custom-call(bf16[3,100,1000]{2,1,0:T(8,128)(2,1)} %bitcast.21, bf16[3,1000,1000]{2,1,0:T(8,128)(2,1)} %bitcast.20, bf16[3,64,100]{2,1,0:T(8,128)(2,1)} %bitcast.22, bf16[3,100,12500]{2,1,0:T(8,128)(2,1)} %cyc_ints.1), custom_call_target="tpu_custom_call" | custom-call | flops 5280000000 | bytes 13500000 | tf_op jit(solution)/shard_map/residual/pallas_call | solution.py:414
  75.0 1.7 %reshape.145 = f32[8,2,13312]{2,1,0:T(2,128)S(1)} reshape(f32[8,16,1664]{2,1,0:T(8,128)} %get-tuple-element.8) | data formatting | bytes 1703936 | tf_op jit(solution)/shard_map/reshape | solution.py:467
  76.6 0.1 slice.20
  76.7 0.1 copy.19
  76.8 0.4 reshape.146
  78.5 0.0 copy-done
  78.5 0.6 dynamic_slice.7
  79.1 0.0 copy-done.1
  79.1 0.7 dynamic-slice_subtract_fusion
  79.8 0.1 broadcast_add_fusion
  79.9 0.0 copy-done.2
  79.9 0.2 reduce-window.9
  80.1 0.6 fusion.1
  80.7 0.1 convert_reduce_fusion
  80.8 0.0 copy-done.3
  80.8 0.2 reduce-window.6
  81.0 0.1 convert_reduce_fusion.1
  81.1 0.1 broadcast_xor_fusion
  81.2 0.2 fusion
  81.4 0.6 broadcast_xor_fusion.1
  82.1 1.5 %select_bitcast_fusion = f32[2,1,100,1000]{3,2,0,1:T(8,128)S(1)} fusion(f32[2,100,1000]{2,1,0:T(8,128)S(1)} %reshape.146, f32[2,112,1024]{2,1,0:T(8,128)} %get-tuple-element.7, f32[1000]{0:T(1024)S(1)} %copy-done, f32[2,100]{1,0:T(2,128)S(1)} %broadcast_add_fusion, s32[100,1000]{1,0:T(8,128)S(1)} %broadcast_xor_fusion, s32[2]{0:T(128)S(1)} %broadcast_xor_fusion.1), kind=kLoop, calls=%fused_computation | loop fusion | flops 1200000 | bytes 2804808 | tf_op jit(solution)/shard_map/jit(_where)/select_n | solution.py:489
  83.6 1.7 %copy.16 = f32[2,1,100,1000]{3,1,2,0:T(1,128)} copy(f32[2,1,100,1000]{3,2,0,1:T(8,128)S(1)} %select_bitcast_fusion) | data formatting | bytes 1600000 | tf_op jit(solution)/shard_map/jit(_where)/select_n | solution.py:489
  (2 shorter events, 0.0 us)
Async XLA Ops:
  0.0 78.5 %copy-start = (f32[1000]{0:T(1024)S(1)}, f32[1000]{0:T(1024)}, u32[]{:S(2)}) copy-start(f32[1000]{0:T(1024)} %param.19) | copy-start | bytes 12004
  0.0 79.1 %copy-start.1 = (f32[100]{0:T(128)S(1)}, f32[100]{0:T(128)}, u32[]{:S(2)}) copy-start(f32[100]{0:T(128)} %param.18) | copy-start | bytes 1204
  0.0 79.9 %copy-start.2 = (s32[8]{0:T(128)S(1)}, s32[8]{0:T(128)}, u32[]{:S(2)}) copy-start(s32[8]{0:T(128)} %param.15) | copy-start | bytes 100
  0.0 80.8 %copy-start.3 = (s32[8]{0:T(128)S(1)}, s32[8]{0:T(128)}, u32[]{:S(2)}) copy-start(s32[8]{0:T(128)} %param.14) | copy-start | bytes 100

commit v3 on v2

--- a/solution.py
+++ b/solution.py
@@ -203,7 +203,6 @@
     b_copy.wait()
     for c in range(depth):
         gat[v, c] = a_buf[c, 0:base, :]
-    multiply(v)
 
     def t_hop(t):
         to = (v + t) % n_v
@@ -262,6 +261,20 @@
                 for h in x_hops(nz - 1 + d, z + d, c):
                     h.start()
 
+            if d == 1:
+                if c == 0:
+                    multiply(v)
+            else:
+                back = d - 1
+
+                @pl.when((z - back >= 0) if c % 2 == 0 else (z + back < nz))
+                def _():
+                    zb = z - back if c % 2 == 0 else z + back
+                    if c < 2:
+                        multiply(zb * nx + x)
+                    elif c < 4:
+                        take_row(zb)
+
         if d == min(2, nz - 1):
             cycle_exchange()
         if d == 1:
@@ -285,30 +298,16 @@
                 return 0
 
             lax.fori_loop(1, nx, one, 0)
-        else:
-            @pl.when(z - (d - 1) >= 0)
-            def _():
-                take_row(z - (d - 1))
-
-            @pl.when(z + (d - 1) < nz)
-            def _():
-                take_row(z + (d - 1))
-
-        @pl.when(z - d >= 0)
-        def _():
-            multiply((z - d) * nx + x)
-
-        @pl.when(z + d < nz)
-        def _():
-            multiply((z + d) * nx + x)
-
-    @pl.when(z - (nz - 1) >= 0)
+
+    far = nz - 1
+
+    @pl.when(z - far >= 0)
     def _():
-        take_row(z - (nz - 1))
-
-    @pl.when(z + (nz - 1) < nz)
+        multiply((z - far) * nx + x)
+
+    @pl.when(z + far < nz)
     def _():
-        take_row(z + (nz - 1))
+        multiply((z + far) * nx + x)
 
     cyc_out[v] = tile[v]
     for t in range(1, n_v):
@@ -317,6 +316,14 @@
         got = arecv[src]
         e = got[:, ch - 128:].astype(jnp.float32)[I_DEV * Q - 1:I_DEV * Q, 127:128]
         cyc_out[src] = decode(got, e)
+
+    @pl.when(z - far >= 0)
+    def _():
+        take_row(z - far)
+
+    @pl.when(z + far < nz)
+    def _():
+        take_row(z + far)
 
     for s in range(1, n_o):
         src = (o + s) % n_o

time: 85.6 us -> 86.1 us (level)
  no operation moved by 1% of the time
where the time goes in v3:
time: 86.1 us; the launch traced here: 85.8 us
  Pallas kernels  75.4 us (88%)
  local copies, waits for them, and re-layouts  4.56 us (5%)
  other arithmetic  4.41 us (5%)
  between operations  1.42 us (2%)
    pallas_call x1, Pallas kernels, shards(): pl.pallas_call(functools.partial(kernel, n_o, n_v, pairs, pairs_pad, dept...  75.4 us
    reshape x2, local copies, waits for them, and re-layouts, shards(): cyc.reshape(n_v, I_DEV, Q * ch)[:, :, :jb].transpose(1, 0, 2)  2.11 us
    select_n x1, local copies, waits for them, and re-layouts, shards(): return jnp.where(total_sym == 0, resid / denom, jnp.float32(0.0))  1.73 us

profile of v3, /device:TPU:5, one launch (start us, length us, event | category | flops | bytes accessed | tf_op | source)
XLA Modules:
  0.0 85.8 jit_solution(15552734929399997540)
XLA Ops:
  0.0 0.0 copy-start
  0.0 0.0 copy-start.1
  0.0 0.0 copy-start.2
  0.0 0.0 copy-start.3
  0.0 75.4 %residual.1 = (f32[2,112,1024]{2,1,0:T(8,128)}, f32[8,16,1664]{2,1,0:T(8,128)}) custom-call(bf16[3,100,1000]{2,1,0:T(8,128)(2,1)} %bitcast.21, bf16[3,1000,1000]{2,1,0:T(8,128)(2,1)} %bitcast.20, bf16[3,64,100]{2,1,0:T(8,128)(2,1)} %bitcast.22, bf16[3,100,12500]{2,1,0:T(8,128)(2,1)} %cyc_ints.1), custom_call_target="tpu_custom_call" | custom-call | flops 5280000000 | bytes 13500000 | tf_op jit(solution)/shard_map/residual/pallas_call | solution.py:421
  75.4 1.7 %reshape.145 = f32[8,2,13312]{2,1,0:T(2,128)S(1)} reshape(f32[8,16,1664]{2,1,0:T(8,128)} %get-tuple-element.8) | data formatting | bytes 1703936 | tf_op jit(solution)/shard_map/reshape | solution.py:474
  77.1 0.1 slice.20
  77.1 0.1 copy.19
  77.2 0.4 reshape.146
  79.0 0.0 copy-done
  79.0 0.6 dynamic_slice.7
  79.6 0.0 copy-done.1
  79.6 0.7 dynamic-slice_subtract_fusion
  80.3 0.1 broadcast_add_fusion
  80.4 0.0 copy-done.2
  80.4 0.2 reduce-window.9
  80.5 0.6 fusion.1
  81.2 0.1 convert_reduce_fusion
  81.3 0.0 copy-done.3
  81.3 0.2 reduce-window.6
  81.5 0.1 convert_reduce_fusion.1
  81.6 0.1 broadcast_xor_fusion
  81.7 0.2 fusion
  81.9 0.6 broadcast_xor_fusion.1
  82.5 1.5 %select_bitcast_fusion = f32[2,1,100,1000]{3,2,0,1:T(8,128)S(1)} fusion(f32[2,100,1000]{2,1,0:T(8,128)S(1)} %reshape.146, f32[2,112,1024]{2,1,0:T(8,128)} %get-tuple-element.7, f32[1000]{0:T(1024)S(1)} %copy-done, f32[2,100]{1,0:T(2,128)S(1)} %broadcast_add_fusion, s32[100,1000]{1,0:T(8,128)S(1)} %broadcast_xor_fusion, s32[2]{0:T(128)S(1)} %broadcast_xor_fusion.1), kind=kLoop, calls=%fused_computation | loop fusion | flops 1200000 | bytes 2804808 | tf_op jit(solution)/shard_map/jit(_where)/select_n | solution.py:496
  84.0 1.7 %copy.16 = f32[2,1,100,1000]{3,1,2,0:T(1,128)} copy(f32[2,1,100,1000]{3,2,0,1:T(8,128)S(1)} %select_bitcast_fusion) | data formatting | bytes 1600000 | tf_op jit(solution)/shard_map/jit(_where)/select_n | solution.py:496
  (2 shorter events, 0.0 us)
Async XLA Ops:
  0.0 79.0 %copy-start = (f32[1000]{0:T(1024)S(1)}, f32[1000]{0:T(1024)}, u32[]{:S(2)}) copy-start(f32[1000]{0:T(1024)} %param.19) | copy-start | bytes 12004
  0.0 79.6 %copy-start.1 = (f32[100]{0:T(128)S(1)}, f32[100]{0:T(128)}, u32[]{:S(2)}) copy-start(f32[100]{0:T(128)} %param.18) | copy-start | bytes 1204
  0.0 80.4 %copy-start.2 = (s32[8]{0:T(128)S(1)}, s32[8]{0:T(128)}, u32[]{:S(2)}) copy-start(s32[8]{0:T(128)} %param.15) | copy-start | bytes 100
  0.0 81.3 %copy-start.3 = (s32[8]{0:T(128)S(1)}, s32[8]{0:T(128)}, u32[]{:S(2)}) copy-start(s32[8]{0:T(128)} %param.14) | copy-start | bytes 100

commit v4 on v2

--- a/solution.py
+++ b/solution.py
@@ -376,8 +376,13 @@
     lax.fori_loop(0, n_v, sent, 0)
 
 
+def picked(values, index):
+    here = index[:, None] == jnp.arange(values.shape[0], dtype=jnp.int32)[None, :]
+    return jnp.sum(jnp.where(here, values[None, :], 0.0), axis=1)
+
+
 def irrep_of(blocks, index):
-    bounds = jnp.cumsum(blocks)[:-1]
+    bounds = jnp.sum(jnp.where(jnp.tri(7, 8, dtype=jnp.bool_), blocks[None, :], 0), axis=1)
     return jnp.sum((index[:, None] >= bounds[None, :]).astype(jnp.int32), axis=1)
 
 
@@ -478,8 +483,8 @@
         jnp.bitwise_xor(sym_i[:, None, None, None], sym_a[None, :, None, None]),
         jnp.bitwise_xor(sym_j[None, None, :, None], sym_b[None, None, None, :]),
     )
-    e_i = lax.dynamic_slice_in_dim(eps_occ, first_occ, I_DEV)
-    e_a = lax.dynamic_slice_in_dim(eps_virt, first_virt, A_DEV)
+    e_i = picked(eps_occ, glob_i)
+    e_a = picked(eps_virt, glob_a)
     denom = (
         e_i[:, None, None, None]
         - e_a[None, :, None, None]

time: 85.6 us -> 85.6 us (level)
    reduce_sum x0 -> x4, other arithmetic: none -> 1.01 us  [the longest x2 0.78 us: picked(): return jnp.sum(jnp.where(here, values[None, :], 0.0), axis=1)]
where the time goes in v4:
time: 85.6 us; the launch traced here: 85.3 us
  Pallas kernels  74.9 us (88%)
  other arithmetic  4.99 us (6%)
  local copies, waits for them, and re-layouts  3.96 us (5%)
  between operations  1.44 us (2%)
    pallas_call x1, Pallas kernels, shards(): pl.pallas_call(functools.partial(kernel, n_o, n_v, pairs, pairs_pad, dept...  74.9 us
    reshape x2, local copies, waits for them, and re-layouts, shards(): cyc.reshape(n_v, I_DEV, Q * ch)[:, :, :jb].transpose(1, 0, 2)  2.11 us
    select_n x1, local copies, waits for them, and re-layouts, shards(): return jnp.where(total_sym == 0, resid / denom, jnp.float32(0.0))  1.73 us

profile of v4, /device:TPU:5, one launch (start us, length us, event | category | flops | bytes accessed | tf_op | source)
XLA Modules:
  0.0 85.3 jit_solution(15231424058850683785)
XLA Ops:
  0.0 0.0 copy-start.1
  0.0 0.0 copy-start
  0.0 0.0 copy-start.2
  0.0 0.0 copy-start.3
  0.0 74.9 %residual.1 = (f32[2,112,1024]{2,1,0:T(8,128)}, f32[8,16,1664]{2,1,0:T(8,128)}) custom-call(bf16[3,100,1000]{2,1,0:T(8,128)(2,1)} %bitcast.14, bf16[3,1000,1000]{2,1,0:T(8,128)(2,1)} %bitcast.13, bf16[3,64,100]{2,1,0:T(8,128)(2,1)} %bitcast.15, bf16[3,100,12500]{2,1,0:T(8,128)(2,1)} %cyc_ints.1), custom_call_target="tpu_custom_call" | custom-call | flops 5280000000 | bytes 13500000 | tf_op jit(solution)/shard_map/residual/pallas_call | solution.py:419
  75.0 1.7 %reshape.129 = f32[8,2,13312]{2,1,0:T(2,128)S(1)} reshape(f32[8,16,1664]{2,1,0:T(8,128)} %get-tuple-element.8) | data formatting | bytes 1703936 | tf_op jit(solution)/shard_map/reshape | solution.py:472
  76.6 0.1 slice.8
  76.7 0.1 copy.19
  76.8 0.4 reshape.130
  77.9 0.0 copy-done.1
  77.9 0.2 fusion.1
  78.7 0.0 copy-done
  78.7 0.6 select_reduce_fusion
  79.3 0.6 broadcast_subtract_fusion
  80.0 0.1 broadcast_add_fusion
  80.1 0.0 copy-done.2
  80.1 0.1 select_reduce_fusion.1
  80.2 0.1 convert_reduce_fusion
  80.3 0.0 copy-done.3
  80.3 0.1 select_reduce_fusion.2
  80.4 0.1 convert_reduce_fusion.1
  80.5 0.1 broadcast_xor_fusion
  80.6 0.2 fusion
  80.8 0.6 fusion.2
  81.4 0.6 broadcast_xor_fusion.1
  82.1 1.5 %select_bitcast_fusion = f32[2,1,100,1000]{3,2,0,1:T(8,128)S(1)} fusion(f32[2,100,1000]{2,1,0:T(8,128)S(1)} %reshape.130, f32[2,112,1024]{2,1,0:T(8,128)} %get-tuple-element.7, f32[1000]{0:T(1024)S(1)} %copy-done, f32[2,100]{1,0:T(2,128)S(1)} %broadcast_add_fusion, s32[100,1000]{1,0:T(8,128)S(1)} %broadcast_xor_fusion, s32[2]{0:T(128)S(1)} %broadcast_xor_fusion.1), kind=kLoop, calls=%fused_computation | loop fusion | flops 1200000 | bytes 2804808 | tf_op jit(solution)/shard_map/jit(_where)/select_n | solution.py:494
  83.6 1.7 %copy.16 = f32[2,1,100,1000]{3,1,2,0:T(1,128)} copy(f32[2,1,100,1000]{3,2,0,1:T(8,128)S(1)} %select_bitcast_fusion) | data formatting | bytes 1600000 | tf_op jit(solution)/shard_map/jit(_where)/select_n | solution.py:494
  (1 shorter events, 0.0 us)
Async XLA Ops:
  0.0 77.9 %copy-start.1 = (f32[100]{0:T(128)S(1)}, f32[100]{0:T(128)}, u32[]{:S(2)}) copy-start(f32[100]{0:T(128)} %param.18) | copy-start | bytes 1204
  0.0 78.7 %copy-start = (f32[1000]{0:T(1024)S(1)}, f32[1000]{0:T(1024)}, u32[]{:S(2)}) copy-start(f32[1000]{0:T(1024)} %param.19) | copy-start | bytes 12004
  0.0 80.1 %copy-start.2 = (s32[8]{0:T(128)S(1)}, s32[8]{0:T(128)}, u32[]{:S(2)}) copy-start(s32[8]{0:T(128)} %param.15) | copy-start | bytes 100
  0.0 80.3 %copy-start.3 = (s32[8]{0:T(128)S(1)}, s32[8]{0:T(128)}, u32[]{:S(2)}) copy-start(s32[8]{0:T(128)} %param.14) | copy-start | bytes 100
